TPU v7x, 32 devices: a whole 2x2x4 slice. The times are simulated.
32 devices in a mesh: groups: 2 (over y), chan: 4 (over z), tm: 2 (over x), band: 2 (over core).
Axes of the slice: x: 2, y: 2, z: 4, core: 2. Of those that a mesh axis runs over, the one named last changes fastest.
Arguments:
- recording: float32 [1024, 2048], P(('groups', 'chan'), 'tm'), parts along dimension 0, may hold values from -460 to 460
- tau_index: int32 [1024], P(('groups', 'chan')), parts along dimension 0, may hold values from 0 to 7
- pair_offset: int32 [4, 4], replicated, may hold values from -1 to 3, as said below
Outputs:
- correlations: float32 [8, 4, 3, 128, 128], P(('groups', 'chan'), None, None, ('tm', 'band')), parts along dimension 0
There are 2 independent parts, one for each index of `groups`. A program takes and returns all parts, laid end to end along the dimension named above; an argument that names none is the same for every part. Nothing has to cross between parts.
Inputs may be any that keep to these rules, and one draw needn't show every extreme that they name: pair_offset[i, q] is an offset of 1 to 3 blocks for q below the row's partner count, and -1 from there on; every row has 1 to 4 partners.
All inputs are finite; a program needn't handle non-finite values.
Results may differ from a plain program's by a relative error of at most 0.006.
Values may be sent and summed in bfloat16 or wider, within the bound.
A program may use at most 64 MiB of HBM per device.

v0:
```python
import math

import jax
import jax.numpy as jnp
from jax import lax
from jax.sharding import PartitionSpec as P

BLK = 128
HALO_CH = 64
HALO_T = 256
LAGS = 3
QMAX = 4


def from_behind(block, axis, distance):
    devices = range(lax.axis_size(axis))
    route = [(i - distance, i) for i in devices if i - distance in devices]
    return lax.ppermute(block, axis, route)


def padded_2(block, sides, width):
    for axis, dim in sides:
        count = lax.axis_size(axis)
        forward = [(i, i + 1) for i in range(count - 1)]
        backward = [(target, source) for source, target in forward]
        low = lax.ppermute(
            lax.slice_in_dim(block, block.shape[dim] - width, None, axis=dim), axis, forward
        )
        high = lax.ppermute(lax.slice_in_dim(block, 0, width, axis=dim), axis, backward)
        block = jnp.concatenate([low, block, high], axis=dim)
    return block


def slide_total(padded, reach, size, axis):
    zero_shape = list(padded.shape)
    zero_shape[axis] = 1
    running = jnp.concatenate(
        [jnp.zeros(zero_shape, jnp.float32), jnp.cumsum(padded, axis=axis)], axis=axis
    )
    upper = lax.slice_in_dim(running, 2 * reach + 1, 2 * reach + 1 + size, axis=axis)
    lower = lax.slice_in_dim(running, 0, size, axis=axis)
    return upper - lower


def spatial_filter(padded, center, counted):
    total = slide_total(padded, HALO_CH, center.shape[0], 0)
    return center - total / counted[:, None]


def amplitude_norm(padded, center):
    total = slide_total(jnp.abs(padded), HALO_T, center.shape[1], 1)
    return center / (total / (2.0 * HALO_T + 1.0) + 1e-06)


def shards(recording, tau_index, pair_offset):
    channels, samples = recording.shape
    chan_count = lax.axis_size("chan")
    time_count = lax.axis_size("tm")
    band_count = lax.axis_size("band")
    chan_pos = lax.axis_index("chan")
    time_pos = lax.axis_index("tm")
    band_pos = lax.axis_index("band")
    all_channels = channels * chan_count
    all_samples = samples * time_count
    kept_bins = all_samples // 4
    first_bin = kept_bins // 4
    band_bins = kept_bins // band_count
    device_bins = band_bins // time_count
    decay = jnp.exp(-1.0 / (2.0 * 2.0 ** (tau_index.astype(jnp.float32) / 2.0)))[:, None]
    rows_global = chan_pos * channels + jnp.arange(channels)
    counted = (
        jnp.minimum(rows_global, HALO_CH) + jnp.minimum(all_channels - 1 - rows_global, HALO_CH) + 1
    ).astype(jnp.float32)
    previous = from_behind(recording[:, samples - 1 :], "tm", 1)
    deconv = recording - decay * jnp.concatenate([previous, recording[:, : samples - 1]], axis=1)
    deconv_wide = padded_2(deconv, (("chan", 0),), HALO_CH)
    filtered = spatial_filter(deconv_wide, deconv, counted)
    filtered_wide = padded_2(filtered, (("tm", 1),), HALO_T)
    normed = amplitude_norm(filtered_wide, filtered)
    time_global = time_pos * samples + jnp.arange(samples)
    sub_rows = math.gcd(device_bins * lax.axis_size("tm"), 128)
    pieces = device_bins * lax.axis_size("tm") // sub_rows

    def one_piece(piece_idx):
        bins_here = first_bin + band_pos * band_bins + piece_idx * sub_rows + jnp.arange(sub_rows)
        turns = bins_here[:, None] * time_global[None, :] % all_samples
        angle = 2.0 * jnp.pi / all_samples * turns.astype(jnp.float32)
        dims = (((1,), (1,)), ((), ()))
        real_part = lax.dot_general(
            jnp.cos(angle),
            normed,
            dims,
            precision=lax.Precision.HIGHEST,
            preferred_element_type=jnp.float32,
        )
        imag_part = -lax.dot_general(
            jnp.sin(angle),
            normed,
            dims,
            precision=lax.Precision.HIGHEST,
            preferred_element_type=jnp.float32,
        )
        return jnp.stack([real_part, imag_part], axis=1)

    stacked = lax.map(one_piece, jnp.arange(pieces))
    spectra = lax.psum_scatter(
        stacked.reshape(device_bins * lax.axis_size("tm"), 2, channels),
        "tm",
        scatter_dimension=0,
        tiled=True,
    )
    local_power = jnp.sum(spectra * spectra, axis=(0, 1))
    power = lax.psum(local_power, ("tm", "band"))
    factor = lax.rsqrt(power / kept_bins + 1e-06)
    white = (spectra * factor[None, None, :]).astype(jnp.bfloat16)
    bins_mine = first_bin + band_pos * band_bins + time_pos * device_bins + jnp.arange(device_bins)
    lagged = jnp.arange(LAGS) - LAGS // 2
    phase = (
        2.0
        * jnp.pi
        / all_samples
        * (bins_mine[:, None] * lagged[None, :] % all_samples).astype(jnp.float32)
    )
    cosine = jnp.cos(phase)[:, :, None]
    sine = jnp.sin(phase)[:, :, None]
    white_f = white.astype(jnp.float32)
    real_shift = white_f[:, 0, None, :] * cosine - white_f[:, 1, None, :] * sine
    imag_shift = white_f[:, 0, None, :] * sine + white_f[:, 1, None, :] * cosine
    shifted = jnp.stack([real_shift, imag_shift], axis=1).astype(jnp.bfloat16)
    own_blocks = channels // BLK
    all_blocks = all_channels // BLK
    my_offsets = lax.dynamic_slice_in_dim(pair_offset, chan_pos * own_blocks, own_blocks, 0)
    left_blocks = [shifted.reshape(2 * device_bins, LAGS * BLK)]
    cc_scale = 1.0 / math.sqrt(kept_bins)
    initial = tuple(
        (jnp.zeros((LAGS * BLK, BLK), jnp.float32) for slot_all in range(own_blocks * QMAX))
    )
    piece = lax.all_gather(white, "chan", axis=2, tiled=True)
    width = piece.shape[2]
    updated = []
    for slot_idx in range(QMAX):
        offset = my_offsets[0, slot_idx]
        partner = (chan_pos * own_blocks + 0 + jnp.maximum(offset, 0)) % all_blocks
        local_col = partner * BLK
        present = (offset >= 0) & (local_col >= 0) & (local_col < width)
        clipped = jnp.clip(local_col, 0, width - BLK)
        right = lax.dynamic_slice_in_dim(piece, clipped, BLK, 2)
        right = right.reshape(2 * device_bins, BLK)

        def compute(previous_value, left=left_blocks[0], right=right):
            product = lax.dot_general(
                left, right, (((0,), (0,)), ((), ())), preferred_element_type=jnp.float32
            )
            return product * cc_scale

        def keep(previous_value):
            return previous_value

        updated.append(lax.cond(present, compute, keep, initial[slot_idx]))
    gathered = tuple(updated)
    stacked_cc = jnp.stack(gathered).reshape(own_blocks, QMAX, LAGS, BLK, BLK)
    return lax.psum_scatter(stacked_cc, ("tm", "band"), scatter_dimension=3, tiled=True)


def solution(mesh):
    return jax.shard_map(
        shards,
        mesh=mesh,
        in_specs=(P(("groups", "chan"), "tm"), P(("groups", "chan")), P()),
        out_specs=P(("groups", "chan"), None, None, ("tm", "band"), None),
        check_vma=False,
    )
```

profile of v0, /device:TPU:0, one launch (start us, length us, event | category | flops | bytes accessed | tf_op | source)
XLA Modules:
  0.0 122.5 jit_solution(3115787574492478725)
XLA Ops:
  6.5 0.9 slice.63
  7.5 4.8 %collective-permute-start = (f32[128,1]{1,0:T(8,128)S(1)}, f32[128,1]{1,0:T(8,128)S(1)}, u32[]{:S(2)}, u32[]{:S(2)}) collective-permute-start(f32[128,1]{1,0:T(8,128)S(1)} %slice.63), channel_id=1, source_target_pairs={{0,2},{1,3},{4,6},{5,7},{8,10},{9,11},{12,14},{13,15},{16,18},{17,... | collective-permute-start | bytes 1544 | tf_op jit(solution)/shard_map/ppermute | solution.py:18
  12.3 0.7 divide_exponential_fusion
  13.0 1.2 collective-permute-done
  14.2 1.4 %fusion.34 = f32[128,1024]{1,0:T(8,128)S(1)} fusion(f32[128,1024]{1,0:T(8,128)} %param.13, f32[128,1023]{1,0:T(8,128)} %bitcast.94, f32[128,1]{1,0:T(8,128)S(1)} %collective-permute-done, f32[128]{0:T(128)S(1)} %divide_exponential_fusion), kind=kLoop, calls=%fused_computation.55 | loop fusion | flops 393216 | bytes 1573376 | tf_op jit(solution)/shard_map/sub | solution.py:75
  15.7 3.5 %collective-permute-start.1 = (f32[64,1024]{1,0:T(8,128)S(1)}, f32[64,1024]{1,0:T(8,128)S(1)}, u32[]{:S(2)}, u32[]{:S(2)}) collective-permute-start(f32[64,1024]{1,0:T(8,128)S(1)} %get-tuple-element.262), channel_id=1, source_target_pairs={{0,4},{4,8},{8,12},{1,5},{5,9},{9,13},{2,6},{6,10},{10,14},{3,7},{... | collective-permute-start | bytes 786440 | tf_op jit(solution)/shard_map/ppermute | solution.py:26
  19.2 1.3 %collective-permute-start.2 = (f32[64,1024]{1,0:T(8,128)S(1)}, f32[64,1024]{1,0:T(8,128)S(1)}, u32[]{:S(2)}, u32[]{:S(2)}) collective-permute-start(f32[64,1024]{1,0:T(8,128)S(1)} %get-tuple-element.263), channel_id=1, source_target_pairs={{4,0},{8,4},{12,8},{5,1},{9,5},{13,9},{6,2},{10,6},{14,10},{7,3},{... | collective-permute-start | bytes 786440 | tf_op jit(solution)/shard_map/ppermute | solution.py:29
  20.5 3.4 %collective-permute-done.1 = f32[64,1024]{1,0:T(8,128)S(1)} collective-permute-done((f32[64,1024]{1,0:T(8,128)S(1)}, f32[64,1024]{1,0:T(8,128)S(1)}, u32[]{:S(2)}, u32[]{:S(2)}) %collective-permute-start.1) | collective-permute-done | bytes 262176 | tf_op jit(solution)/shard_map/ppermute | solution.py:26
  23.9 4.1 %collective-permute-done.2 = f32[64,1024]{1,0:T(8,128)S(1)} collective-permute-done((f32[64,1024]{1,0:T(8,128)S(1)}, f32[64,1024]{1,0:T(8,128)S(1)}, u32[]{:S(2)}, u32[]{:S(2)}) %collective-permute-start.2) | collective-permute-done | bytes 262176 | tf_op jit(solution)/shard_map/ppermute | solution.py:29
  28.1 0.8 fusion.25
  29.6 4.0 %collective-permute-start.3 = (f32[128,256]{1,0:T(8,128)S(1)}, f32[128,256]{1,0:T(8,128)S(1)}, u32[]{:S(2)}, u32[]{:S(2)}) collective-permute-start(f32[128,256]{1,0:T(8,128)S(1)} %get-tuple-element.260), channel_id=1, source_target_pairs={{0,2},{1,3},{4,6},{5,7},{8,10},{9,11},{12,14},{13,15},{16,18},{17,... | collective-permute-start | bytes 393224 | tf_op jit(solution)/shard_map/ppermute | solution.py:26
  33.6 1.3 %collective-permute-start.4 = (f32[128,256]{1,0:T(8,128)S(1)}, f32[128,256]{1,0:T(8,128)S(1)}, u32[]{:S(2)}, u32[]{:S(2)}) collective-permute-start(f32[128,256]{1,0:T(8,128)S(1)} %get-tuple-element.261), channel_id=1, source_target_pairs={{2,0},{3,1},{6,4},{7,5},{10,8},{11,9},{14,12},{15,13},{18,16},{19,... | collective-permute-start | bytes 393224 | tf_op jit(solution)/shard_map/ppermute | solution.py:29
  34.9 1.2 collective-permute-done.3
  36.0 4.4 %collective-permute-done.4 = f32[128,256]{1,0:T(8,128)S(1)} collective-permute-done((f32[128,256]{1,0:T(8,128)S(1)}, f32[128,256]{1,0:T(8,128)S(1)}, u32[]{:S(2)}, u32[]{:S(2)}) %collective-permute-start.4) | collective-permute-done | bytes 131104 | tf_op jit(solution)/shard_map/ppermute | solution.py:29
  42.1 13.2 %while.13 = (s32[]{:T(128)}, f32[2,128,2,128]{3,1,0,2:T(8,128)S(1)}, s32[2]{0:T(128)S(1)}, s32[]{:T(128)}, f32[128,1024]{1,0:T(8,128)S(1)}, /*index=5*/s32[]{:T(128)}, s32[]{:T(128)}, s32[1]{0:T(128)}) while((s32[]{:T(128)}, f32[2,128,2,128]{3,1,0,2:T(8,128)S(1)}, s32[2]{0:T(128)S(1)}, s32[]{:T(128)}, f32[128,1024]{1,0:T(8,128)S(1)}, ...), condition=%wide.region_5.6_spmd.clone, body=%wide.region_4.5_spmd.clone.sunk | while | flops 406373504 | bytes 1455749 | solution.py:105
  43.5 2.6 %convolution_bitcast_fusion.2 = f32[128,1,128]{2,0,1:T(8,128)S(1)} fusion(f32[128,1024]{1,0:T(8,128)S(1)} %get-tuple-element.331, s32[1024]{0:T(1024)S(1)} %iota_add_fusion.6, s32[128]{0:T(128)S(1)} %iota_add_fusion.7), kind=kOutput, calls=%fused_computation.15.clone.1 | convolution fusion | flops 203161600 | bytes 594432 | tf_op jit(solution)/shard_map/while/body/eval_jaxpr/dot_general | solution.py:89
  46.1 2.6 %fusion.64 = f32[128,1,128]{2,0,1:T(8,128)S(1)} fusion(f32[128,1024]{1,0:T(8,128)S(1)} %get-tuple-element.331, s32[1024]{0:T(1024)S(1)} %iota_add_fusion.6, s32[128]{0:T(128)S(1)} %iota_add_fusion.7), kind=kOutput, calls=%fused_computation.14.clone.1 | convolution fusion | flops 203177984 | bytes 594432 | tf_op jit(solution)/shard_map/while/body/eval_jaxpr/dot_general | solution.py:96
  50.1 2.6 %convolution_bitcast_fusion.2 = f32[128,1,128]{2,0,1:T(8,128)S(1)} fusion(f32[128,1024]{1,0:T(8,128)S(1)} %get-tuple-element.331, s32[1024]{0:T(1024)S(1)} %iota_add_fusion.6, s32[128]{0:T(128)S(1)} %iota_add_fusion.7), kind=kOutput, calls=%fused_computation.15.clone.1 | convolution fusion | flops 203161600 | bytes 594432 | tf_op jit(solution)/shard_map/while/body/eval_jaxpr/dot_general | solution.py:89
  52.7 2.6 %fusion.64 = f32[128,1,128]{2,0,1:T(8,128)S(1)} fusion(f32[128,1024]{1,0:T(8,128)S(1)} %get-tuple-element.331, s32[1024]{0:T(1024)S(1)} %iota_add_fusion.6, s32[128]{0:T(128)S(1)} %iota_add_fusion.7), kind=kOutput, calls=%fused_computation.14.clone.1 | convolution fusion | flops 203177984 | bytes 594432 | tf_op jit(solution)/shard_map/while/body/eval_jaxpr/dot_general | solution.py:96
  55.3 0.7 copy-done.1
  56.1 0.7 fusion.43
  62.3 4.9 %reduce-scatter.3.cloned.1.call-done = f32[128,2,128]{2,0,1:T(8,128)} async-done(((f32[256,2,128]{2,0,1:T(8,128)}), f32[128,2,128]{2,0,1:T(8,128)}) %reduce-scatter.3.cloned.1.call-update) | async-done | bytes 131088 | tf_op jit(solution)/shard_map/reduce_scatter | solution.py:106
  67.1 1.0 multiply_reduce_fusion
  68.1 5.8 %psum.7 = f32[128]{0:T(128)S(1)} all-reduce(f32[128]{0:T(128)S(1)} %multiply_reduce_fusion), channel_id=1, replica_groups=mesh['groups'=2,'chan'=4,'tm'=2,'band'=2] {'tm','band'}, use_global_device_ids=true, to_apply=%region_8.9 | all-reduce | flops 128 | bytes 1024 | tf_op jit(solution)/shard_map/psum | solution.py:113
  73.9 0.9 fusion.40
  75.4 13.0 %all_gather.3 = bf16[128,2,512]{2,0,1:T(8,128)(2,1)S(1)} all-gather(bf16[128,2,128]{2,0,1:T(8,128)(2,1)S(1)} %get-tuple-element.259), channel_id=1, replica_groups=mesh['groups'=2,'chan'=4,'tm'=2,'band'=2] {'chan'}, dimensions={2}, use_global_device_ids=true | all-gather | bytes 327680 | tf_op jit(solution)/shard_map/all_gather | solution.py:138
  88.4 0.8 conditional.4
  89.2 0.8 conditional.5
  90.0 0.8 conditional.6
  90.8 0.8 conditional.7
  91.6 1.0 pad_maximum_fusion.1
  92.6 23.1 %reduce-scatter.5.cloned.1.call-done = f32[1,4,3,32,128]{4,3,2,1,0:T(8,128)} async-done(((f32[1,4,3,128,128]{4,3,2,1,0:T(8,128)}), f32[1,4,3,32,128]{4,3,2,1,0:T(8,128)}) %reduce-scatter.5.cloned.1.call-update) | async-done | bytes 196624 | tf_op jit(solution)/shard_map/reduce_scatter | solution.py:162
  (64 shorter events, 7.8 us)
Async XLA Ops:
  6.5 28.3 %copy-start = (s32[4,4]{1,0:T(4,128)S(1)}, s32[4,4]{1,0:T(4,128)}, u32[]{:S(2)}) copy-start(s32[4,4]{1,0:T(4,128)} %param.15) | copy-start | bytes 196
  6.5 60.6 %reduce-scatter.3.cloned.1.call-start = ((), (), s32[]{:S(2)}) async-start(), calls=%async_computation.2 | async-start | bytes 393216 | tf_op jit(solution)/shard_map/reduce_scatter | solution.py:106
  7.5 6.7 %collective-permute-start = (f32[128,1]{1,0:T(8,128)S(1)}, f32[128,1]{1,0:T(8,128)S(1)}, u32[]{:S(2)}, u32[]{:S(2)}) collective-permute-start(f32[128,1]{1,0:T(8,128)S(1)} %slice.63), channel_id=1, source_target_pairs={{0,2},{1,3},{4,6},{5,7},{8,10},{9,11},{12,14},{13,15},{16,18},{17,... | collective-permute-start | bytes 1544 | tf_op jit(solution)/shard_map/ppermute | solution.py:18
  15.7 8.2 %collective-permute-start.1 = (f32[64,1024]{1,0:T(8,128)S(1)}, f32[64,1024]{1,0:T(8,128)S(1)}, u32[]{:S(2)}, u32[]{:S(2)}) collective-permute-start(f32[64,1024]{1,0:T(8,128)S(1)} %get-tuple-element.262), channel_id=1, source_target_pairs={{0,4},{4,8},{8,12},{1,5},{5,9},{9,13},{2,6},{6,10},{10,14},{3,7},{... | collective-permute-start | bytes 786440 | tf_op jit(solution)/shard_map/ppermute | solution.py:26
  19.2 8.8 %collective-permute-start.2 = (f32[64,1024]{1,0:T(8,128)S(1)}, f32[64,1024]{1,0:T(8,128)S(1)}, u32[]{:S(2)}, u32[]{:S(2)}) collective-permute-start(f32[64,1024]{1,0:T(8,128)S(1)} %get-tuple-element.263), channel_id=1, source_target_pairs={{4,0},{8,4},{12,8},{5,1},{9,5},{13,9},{6,2},{10,6},{14,10},{7,3},{... | collective-permute-start | bytes 786440 | tf_op jit(solution)/shard_map/ppermute | solution.py:29
  29.6 6.5 %collective-permute-start.3 = (f32[128,256]{1,0:T(8,128)S(1)}, f32[128,256]{1,0:T(8,128)S(1)}, u32[]{:S(2)}, u32[]{:S(2)}) collective-permute-start(f32[128,256]{1,0:T(8,128)S(1)} %get-tuple-element.260), channel_id=1, source_target_pairs={{0,2},{1,3},{4,6},{5,7},{8,10},{9,11},{12,14},{13,15},{16,18},{17,... | collective-permute-start | bytes 393224 | tf_op jit(solution)/shard_map/ppermute | solution.py:26
  33.6 6.9 %collective-permute-start.4 = (f32[128,256]{1,0:T(8,128)S(1)}, f32[128,256]{1,0:T(8,128)S(1)}, u32[]{:S(2)}, u32[]{:S(2)}) collective-permute-start(f32[128,256]{1,0:T(8,128)S(1)} %get-tuple-element.261), channel_id=1, source_target_pairs={{2,0},{3,1},{6,4},{7,5},{10,8},{11,9},{14,12},{15,13},{18,16},{19,... | collective-permute-start | bytes 393224 | tf_op jit(solution)/shard_map/ppermute | solution.py:29
  55.3 0.7 copy-start.1
  56.0 59.6 %reduce-scatter.5.cloned.1.call-start = ((), (), s32[]{:S(2)}) async-start(), calls=%async_computation.3 | async-start | bytes 983040 | tf_op jit(solution)/shard_map/reduce_scatter | solution.py:162
Sparse Core Ops, SparseCore 0:
  56.1 10.9 reduce-scatter.2
  92.7 22.9 reduce-scatter.4
where the time goes:
time: 123 us
  waiting for transfers between devices  42.2 us (34%)
  between operations  18.9 us (15%)
  blocking collectives  18.8 us (15%)
  starting transfers between devices  14.9 us (12%)
  matrix products  11.1 us (9%)
  other arithmetic  7.66 us (6%)
  local copies, waits for them, and re-layouts  7.27 us (6%)
  loops' own time  1.66 us (1%)
    reduce_scatter x1, waiting for transfers between devices, shards(): lax.psum_scatter(stacked_cc, ('tm', 'band'), scatter_dimension=3, tiled=T...  23.1 us
    all_gather x1, blocking collectives, shards(): piece = lax.all_gather(white, 'chan', axis=2, tiled=True)  13 us
    ppermute x2, waiting for transfers between devices, padded_2(): lax.ppermute(lax.slice_in_dim(block, 0, width, axis=dim), axis, backward)  8.49 us
    ppermute x2, starting transfers between devices, padded_2(): lax.ppermute(lax.slice_in_dim(block, block.shape[dim] - width, None, axis...  7.47 us
    psum x1, blocking collectives, shards(): power = lax.psum(local_power, ('tm', 'band'))  5.75 us
    dot_general x2, matrix products, one_piece(): lax.dot_general(jnp.sin(angle), normed, dims, precision=lax.Precision.HIG...  5.16 us
    dot_general x2, matrix products, one_piece(): lax.dot_general(jnp.cos(angle), normed, dims, precision=lax.Precision.HIG...  5.13 us
    reduce_scatter x1, waiting for transfers between devices, shards(): lax.psum_scatter(stacked.reshape(device_bins * lax.axis_size('tm'), 2, ch...  4.85 us
  transfers between devices with their start and end apart: 7, of which 7 were waited for; matrix products, arithmetic and copies ran while one was open for 1% of the time, Pallas kernels for 0%

commit v1 on v0

v1 whole, which is shorter than its diff:
```python
import functools
import math

import jax
import jax.numpy as jnp
import ml_dtypes
import numpy as np
from jax import lax
from jax.experimental import pallas as pl
from jax.experimental.pallas import tpu as pltpu
from jax.sharding import PartitionSpec as P

BLK = 128
HALO_CH = 64
HALO_T = 256
LAGS = 3
QMAX = 4
WIN = 2 * HALO_T + 1
OUT_T = 256
BF = jnp.bfloat16
F32 = jnp.float32
NT = (((1,), (1,)), ((), ()))


def tables(samples, all_samples):
    kept = all_samples // 4
    first = kept // 4
    shares = all_samples // samples
    bins = first + np.arange(kept)
    angle = 2.0 * np.pi / all_samples * (np.arange(samples)[:, None] * bins[None, :] % all_samples)
    full = np.concatenate([np.cos(angle), -np.sin(angle)], axis=1).astype(np.float32)
    high = full.astype(ml_dtypes.bfloat16)
    low = (full - high.astype(np.float32)).astype(ml_dtypes.bfloat16)
    turn = 2.0 * np.pi / shares * (np.arange(shares)[:, None] * bins[None, :] % shares)
    share_phase = np.stack([np.cos(turn), np.sin(turn)], axis=1).astype(np.float32)
    lags = np.arange(LAGS) - LAGS // 2
    phase = 2.0 * np.pi / all_samples * (lags[:, None] * bins[None, :] % all_samples)
    lag_phase = np.stack([np.cos(phase), np.sin(phase)], axis=1).astype(np.float32)
    return np.stack([high, low]), share_phase, lag_phase


def split(x):
    high = x.astype(BF)
    return high, (x - high.astype(F32)).astype(BF)


def dot(a, b):
    return jnp.dot(a, b, preferred_element_type=F32)


def kernel(
    C, T, B,
    rec, tau, pair, table_hbm, share_phase, lag_phase, out,
    table, deconv, halo, g_send, g_own, g_halo, wide, filt, spec, parts, white,
    table_sem, send_sem, halo_sem, time_sem, part_sem, z_sem, x_sem, c_sem,
):
    samples = rec.shape[1]
    half = BLK // B
    rows = BLK // (T * B)
    kept = spec.shape[1] // 2
    c = lax.axis_index("chan")
    t = lax.axis_index("tm")
    b = lax.axis_index("band")
    sends = []
    used = [0]

    def remote(src, dst, recv, where, cond=None, at=None):
        if at is None:
            at = used[0]
            used[0] += 1
        copy = pltpu.make_async_remote_copy(
            src_ref=src, dst_ref=dst, send_sem=send_sem.at[at], recv_sem=recv,
            device_id=where, device_id_type=pl.DeviceIdType.MESH,
        )
        return copy, cond

    def start(*args, **kw):
        copy, cond = remote(*args, **kw)
        sends.append((copy, cond))
        if cond is None:
            copy.start()
        else:
            pl.when(cond)(copy.start)

    def arrived(src, dst, recv, cond=None):
        copy, _ = remote(src, dst, recv, {"band": 1 - b}, at=0)
        if cond is None:
            copy.wait_recv()
        else:
            pl.when(cond)(copy.wait_recv)

    fetch = pltpu.make_async_copy(table_hbm, table, table_sem)
    fetch.start()

    barrier = pltpu.get_barrier_semaphore()
    peers = 0
    for dc in range(C):
        for dt in range(T):
            for db in range(B):
                same = dc == 0 and (dt or db)
                line = dc != 0 and dt == 0 and db == 0
                corner = dc in (1, C - 1) and dt in (1, T - 1) and db == 0
                if not (same or line or (corner and dc != 0 and dt != 0)):
                    continue
                peers += 1
                pl.semaphore_signal(
                    barrier, inc=1,
                    device_id={
                        "chan": lax.rem(c + dc, C), "tm": lax.rem(t + dt, T), "band": lax.rem(b + db, B)
                    },
                    device_id_type=pl.DeviceIdType.MESH,
                )

    tau_row = 2.0 * jnp.exp(tau[...].astype(F32) * (0.5 * math.log(2.0)))
    decay = jnp.transpose(jnp.broadcast_to(jnp.exp(-1.0 / tau_row), (BLK, BLK)))
    lane = lax.broadcasted_iota(jnp.int32, (BLK, BLK), 1)
    last = rec[:, samples - BLK :]
    g_send[...] = jnp.transpose(decay * last)[BLK - 8 :, :]
    decay_wide = jnp.concatenate([decay] * (samples // BLK), axis=1)
    x = rec[...]
    before = pltpu.roll(x, 1, 1)
    first_col = lax.broadcasted_iota(jnp.int32, x.shape, 1) == 0
    deconv[...] = x - jnp.where(first_col, 0.0, decay_wide * before)

    pl.semaphore_wait(barrier, peers)

    step = 1 - 2 * b
    to_chan = c + step
    from_chan = c - step
    has_to = (to_chan >= 0) & (to_chan < C)
    has_from = (from_chan >= 0) & (from_chan < C)
    to_safe = jnp.clip(to_chan, 0, C - 1)
    near = pl.ds(pl.multiple_of((1 - b) * half, half), half)
    start(deconv.at[near], halo, halo_sem.at[0], {"chan": to_safe}, has_to)
    t_next = jnp.minimum(t + 1, T - 1)
    t_prev = jnp.maximum(t - 1, 0)
    has_next = t < T - 1
    has_prev = t > 0
    start(g_send, g_own, halo_sem.at[1], {"tm": t_next}, has_next)
    start(g_send, g_halo, halo_sem.at[2], {"tm": t_next, "chan": to_safe}, has_next & has_to)

    i_own = lax.broadcasted_iota(jnp.int32, (half, BLK), 0) + b * half
    j_own = lax.broadcasted_iota(jnp.int32, (half, BLK), 1)
    near_own = (jnp.abs(i_own - j_own) <= HALO_CH).astype(F32).astype(BF)
    i_h = lax.broadcasted_iota(jnp.int32, (half, half), 0)
    j_h = lax.broadcasted_iota(jnp.int32, (half, half), 1)
    near_halo = (((j_h - i_h) * step) >= 0).astype(F32).astype(BF)
    m = lax.broadcasted_iota(jnp.int32, (OUT_T + 2 * HALO_T, OUT_T), 0)
    o = lax.broadcasted_iota(jnp.int32, (OUT_T + 2 * HALO_T, OUT_T), 1)
    window = ((m >= o) & (m <= o + 2 * HALO_T)).astype(F32).astype(BF)
    all_channels = BLK * C
    r_global = lax.broadcasted_iota(jnp.int32, (half, samples), 0) + c * BLK + b * half
    counted = jnp.minimum(r_global, HALO_CH) + jnp.minimum(all_channels - 1 - r_global, HALO_CH) + 1
    per_count = 1.0 / counted.astype(F32)

    @pl.when(jnp.logical_not(has_from))
    def _():
        halo[...] = jnp.zeros_like(halo)

    @pl.when(jnp.logical_not(has_prev))
    def _():
        g_own[...] = jnp.zeros_like(g_own)
        wide[:, :HALO_T] = jnp.zeros((half, HALO_T), BF)

    @pl.when(jnp.logical_not(has_prev & has_from))
    def _():
        g_halo[...] = jnp.zeros_like(g_halo)

    @pl.when(jnp.logical_not(has_next))
    def _():
        wide[:, HALO_T + samples :] = jnp.zeros((half, HALO_T), BF)

    arrived(g_send, g_own, halo_sem.at[1], has_prev)
    arrived(g_send, g_halo, halo_sem.at[2], has_prev & has_from)
    lane0 = lane == 0

    def column(g):
        return jnp.where(lane0, jnp.transpose(jnp.broadcast_to(g[7:8, :], (BLK, BLK))), 0.0)

    fix_own = column(g_own[...])
    fix_halo_all = column(g_halo[...])
    fix_halo = jnp.where(b == 0, fix_halo_all[half:, :], fix_halo_all[:half, :])
    d = deconv[...]
    d = jnp.concatenate([d[:, :BLK] - fix_own, d[:, BLK:]], axis=1)
    d_high, d_low = split(d)
    total = dot(near_own, d_high) + dot(near_own, d_low)
    mine = jnp.where(b == 0, d[:half], d[half:])

    arrived(deconv.at[near], halo, halo_sem.at[0], has_from)
    h = halo[...]
    h = jnp.concatenate([h[:, :BLK] - fix_halo, h[:, BLK:]], axis=1)
    h_high, h_low = split(h)
    total = total + dot(near_halo, h_high) + dot(near_halo, h_low)
    filtered = mine - total * per_count
    filt[...] = filtered
    wide[:, HALO_T : HALO_T + samples] = jnp.abs(filtered).astype(BF)

    start(
        wide.at[:, pl.ds(samples, HALO_T)], wide.at[:, pl.ds(0, HALO_T)],
        time_sem.at[0], {"tm": t_next}, has_next,
    )
    start(
        wide.at[:, pl.ds(HALO_T, HALO_T)], wide.at[:, pl.ds(HALO_T + samples, HALO_T)],
        time_sem.at[1], {"tm": t_prev}, has_prev,
    )

    def normed_block(n):
        at = n * OUT_T
        amp = dot(wide[:, at : at + OUT_T + 2 * HALO_T], window)
        return filt[:, at : at + OUT_T] / (amp * (1.0 / WIN) + 1e-06)

    blocks = samples // OUT_T
    inner = [normed_block(n) for n in range(1, blocks - 1)]
    fetch.wait()
    arrived(
        wide.at[:, pl.ds(samples, HALO_T)], wide.at[:, pl.ds(0, HALO_T)], time_sem.at[0], has_prev
    )
    arrived(
        wide.at[:, pl.ds(HALO_T, HALO_T)], wide.at[:, pl.ds(HALO_T + samples, HALO_T)],
        time_sem.at[1], has_next,
    )
    normed = jnp.concatenate([normed_block(0)] + inner + [normed_block(blocks - 1)], axis=1)
    n_high, n_low = split(normed)
    both = dot(jnp.concatenate([n_high, n_low], axis=0), table[0])
    spectrum = both[:half] + both[half:] + dot(n_high, table[1])
    cos_t = share_phase[t, 0:1, :]
    sin_t = share_phase[t, 1:2, :]
    re, im = spectrum[:, :kept], spectrum[:, kept:]
    spec[:, :kept] = (re * cos_t + im * sin_t).astype(BF)
    spec[:, kept:] = (im * cos_t - re * sin_t).astype(BF)

    for n in range(T):
        piece = b * T + n
        t_own, b_own = lax.div(piece, B), lax.rem(piece, B)
        me = (t_own == t) & (b_own == b)

        @pl.when(me)
        def _():
            parts[t] = spec[n * rows : (n + 1) * rows, :]

        start(
            spec.at[pl.ds(n * rows, rows)], parts.at[t], part_sem.at[t],
            {"tm": t_own, "band": b_own}, jnp.logical_not(me),
        )
    own = t * B + b
    b_from = lax.div(own, T)
    for n in range(T):
        arrived(
            spec.at[pl.ds(0, rows)], parts.at[n], part_sem.at[n],
            jnp.logical_not((t == n) & (b_from == b)),
        )
    spectra = parts[0].astype(F32)
    for n in range(1, T):
        spectra = spectra + parts[n].astype(F32)
    power = jnp.sum(spectra * spectra, axis=1, keepdims=True)
    mine_white = (spectra * lax.rsqrt(power * (1.0 / kept) + 1e-06)).astype(BF)
    white[c, own] = mine_white

    order = [d for pair_d in zip(range(1, C), range(C - 1, 0, -1)) for d in pair_d]
    order = list(dict.fromkeys(order))
    for dc in order:
        start(white.at[c, own], white.at[c, own], z_sem.at[c], {"chan": lax.rem(c + dc, C)})
    w = mine_white.astype(F32)
    wr, wi = w[:, :kept], w[:, kept:]
    left = []
    for lag in range(LAGS):
        cos_l = lag_phase[lag, 0:1, :]
        sin_l = lag_phase[lag, 1:2, :]
        left.append(jnp.concatenate([wr * cos_l - wi * sin_l, wr * sin_l + wi * cos_l], axis=1))
    left = jnp.concatenate(left, axis=0).astype(BF)
    for dc in order:
        p = lax.rem(c + dc, C)
        arrived(white.at[p, own], white.at[p, own], z_sem.at[p])
        for dt in range(1, T):
            start(
                white.at[p, own], white.at[p, own], x_sem.at[p, t], {"tm": lax.rem(t + dt, T)}
            )
        start(white.at[p, own], white.at[p, own], c_sem.at[p, t], {"band": 1 - b})
    for dc in order:
        p = lax.rem(c + dc, C)
        for dt in range(1, T):
            tt = lax.rem(t + dt, T)
            at = tt * B + b
            arrived(white.at[p, at], white.at[p, at], x_sem.at[p, tt])
            start(white.at[p, at], white.at[p, at], c_sem.at[p, tt], {"band": 1 - b})
    for dc in order:
        p = lax.rem(c + dc, C)
        for tt in range(T):
            at = tt * B + (1 - b)
            arrived(white.at[p, at], white.at[p, at], c_sem.at[p, tt])

    scale = 1.0 / math.sqrt(kept)
    for q in range(QMAX):
        offset = pair[c, q]
        present = offset >= 0
        p = lax.rem(c + jnp.where(present, offset, 1), C)
        right = white[p].reshape(BLK, 2 * kept)
        product = lax.dot_general(left, right, NT, preferred_element_type=F32)
        product = jnp.where(present, product * scale, 0.0)
        for lag in range(LAGS):
            out[0, q, lag] = product[lag * rows : (lag + 1) * rows]

    for copy, cond in sends:
        if cond is None:
            copy.wait_send()
        else:
            pl.when(cond)(copy.wait_send)


def shards(recording, tau_index, pair_offset):
    channels, samples = recording.shape
    C = lax.axis_size("chan")
    T = lax.axis_size("tm")
    B = lax.axis_size("band")
    all_samples = samples * T
    kept = all_samples // 4
    half = BLK // B
    rows = BLK // (T * B)
    table, share_phase, lag_phase = tables(samples, all_samples)
    vmem = pl.BlockSpec(memory_space=pltpu.VMEM)
    n_send = 3 + 2 + T + (C - 1) * (1 + T + T) + 4
    need = table.nbytes + C * BLK * 2 * kept * 2
    return pl.pallas_call(
        functools.partial(kernel, C, T, B),
        out_shape=jax.ShapeDtypeStruct((1, QMAX, LAGS, rows, BLK), F32),
        in_specs=[
            vmem, vmem, pl.BlockSpec(memory_space=pltpu.SMEM),
            pl.BlockSpec(memory_space=pl.ANY), vmem, vmem,
        ],
        out_specs=vmem,
        scratch_shapes=[
            pltpu.VMEM(table.shape, BF),
            pltpu.VMEM((BLK, samples), F32),
            pltpu.VMEM((half, samples), F32),
            pltpu.VMEM((8, BLK), F32),
            pltpu.VMEM((8, BLK), F32),
            pltpu.VMEM((8, BLK), F32),
            pltpu.VMEM((half, samples + 2 * HALO_T), BF),
            pltpu.VMEM((half, samples), F32),
            pltpu.VMEM((half, 2 * kept), BF),
            pltpu.VMEM((T, rows, 2 * kept), BF),
            pltpu.VMEM((C, T * B, rows, 2 * kept), BF),
            pltpu.SemaphoreType.DMA,
            pltpu.SemaphoreType.DMA((n_send,)),
            pltpu.SemaphoreType.DMA((3,)),
            pltpu.SemaphoreType.DMA((2,)),
            pltpu.SemaphoreType.DMA((T,)),
            pltpu.SemaphoreType.DMA((C,)),
            pltpu.SemaphoreType.DMA((C, T)),
            pltpu.SemaphoreType.DMA((C, T)),
        ],
        compiler_params=pltpu.CompilerParams(
            collective_id=0, has_side_effects=True, vmem_limit_bytes=need + (20 << 20)
        ),
    )(
        recording, tau_index.reshape(1, channels), pair_offset,
        jnp.asarray(table), jnp.asarray(share_phase), jnp.asarray(lag_phase),
    )


def solution(mesh):
    return jax.shard_map(
        shards,
        mesh=mesh,
        in_specs=(P(("groups", "chan"), "tm"), P(("groups", "chan")), P()),
        out_specs=P(("groups", "chan"), None, None, ("tm", "band"), None),
        check_vma=False,
    )
```

time: 123 us -> 39.9 us (0.32)
  the two profiles are of different devices: /device:TPU:0 before, /device:TPU:3 now
where the time goes in v1:
time: 39.9 us; the launch traced here: 39.5 us
  Pallas kernels  32.9 us (82%)
  local copies, waits for them, and re-layouts  6.65 us (17%)
    pallas_call x1, Pallas kernels, shards(): pl.pallas_call(functools.partial(kernel, C, T, B), out_shape=jax.ShapeDty...  32.9 us
    unnamed x13, local copies, waits for them, and re-layouts  6.65 us

profile of v1, /device:TPU:3, one launch (start us, length us, event | category | flops | bytes accessed | tf_op | source)
XLA Modules:
  0.0 39.5 jit_solution(10286576288565891676)
XLA Ops:
  0.0 0.0 copy-start
  0.0 2.2 %copy-done = bf16[2,1024,1024]{2,1,0:T(8,128)(2,1)S(1)} copy-done((bf16[2,1024,1024]{2,1,0:T(8,128)(2,1)S(1)}, bf16[2,1024,1024]{2,1,0:T(8,128)(2,1)}, u32[]{:S(2)}) %copy-start) | copy-done | bytes 4194328
  2.2 0.0 copy-start.1
  2.2 1.0 %copy-done.1 = f32[128,1024]{1,0:T(8,128)S(1)} copy-done((f32[128,1024]{1,0:T(8,128)S(1)}, f32[128,1024]{1,0:T(8,128)}, u32[]{:S(2)}) %copy-start.1) | copy-done | bytes 524312
  3.2 0.0 copy-start.2
  3.2 0.7 %copy-done.2 = f32[3,2,512]{2,1,0:T(2,128)S(1)} copy-done((f32[3,2,512]{2,1,0:T(2,128)S(1)}, f32[3,2,512]{2,1,0:T(2,128)}, u32[]{:S(2)}) %copy-start.2) | copy-done | bytes 12312
  3.9 0.0 copy-start.3
  3.9 0.7 %copy-done.3 = f32[2,2,512]{2,1,0:T(2,128)S(1)} copy-done((f32[2,2,512]{2,1,0:T(2,128)S(1)}, f32[2,2,512]{2,1,0:T(2,128)}, u32[]{:S(2)}) %copy-start.3) | copy-done | bytes 8216
  4.6 0.0 copy-start.4
  4.6 0.7 %copy-done.4 = s32[4,4]{1,0:T(4,128)S(1)} copy-done((s32[4,4]{1,0:T(4,128)S(1)}, s32[4,4]{1,0:T(4,128)}, u32[]{:S(2)}) %copy-start.4) | copy-done | bytes 88
  5.3 0.0 copy-start.5
  5.3 0.7 %copy-done.5 = s32[128]{0:T(128)S(1)} copy-done((s32[128]{0:T(128)S(1)}, s32[128]{0:T(128)}, u32[]{:S(2)}) %copy-start.5) | copy-done | bytes 536
  6.0 32.9 %shard_map.64 = f32[1,4,3,32,128]{4,3,2,1,0:T(8,128)S(1)} custom-call(f32[128,1024]{1,0:T(8,128)S(1)} %copy-done.1, s32[1,128]{1,0:T(1,128)S(1)} %bitcast.1, s32[4,4]{1,0:T(4,128)S(1)} %copy-done.4, bf16[2,1024,1024]{2,1,0:T(8,128)(2,1)S(1)} %copy-done, f32[2,2,512]{2,1,0:T(2,128)S(1)} %copy-done.3, f32[3,2,512]{2,1,0:T(2,128)S(1)} %copy-done.2), custom_call_target="tpu_custom_call" | custom-call | tf_op jit(solution)/shard_map/pallas_call | solution.py:323
  38.8 0.7 %copy.8 = f32[1,4,3,32,128]{4,3,2,1,0:T(8,128)} copy(f32[1,4,3,32,128]{4,3,2,1,0:T(8,128)S(1)} %shard_map.64) | data formatting | bytes 393216
Async XLA Ops:
  0.0 2.2 %copy-start = (bf16[2,1024,1024]{2,1,0:T(8,128)(2,1)S(1)}, bf16[2,1024,1024]{2,1,0:T(8,128)(2,1)}, u32[]{:S(2)}) copy-start(bf16[2,1024,1024]{2,1,0:T(8,128)(2,1)} %constant.6.clone.table_hbm) | copy-start | bytes 12582916
  2.2 1.0 %copy-start.1 = (f32[128,1024]{1,0:T(8,128)S(1)}, f32[128,1024]{1,0:T(8,128)}, u32[]{:S(2)}) copy-start(f32[128,1024]{1,0:T(8,128)} %rec.1) | copy-start | bytes 1572868
  3.2 0.7 %copy-start.2 = (f32[3,2,512]{2,1,0:T(2,128)S(1)}, f32[3,2,512]{2,1,0:T(2,128)}, u32[]{:S(2)}) copy-start(f32[3,2,512]{2,1,0:T(2,128)} %constant.8.clone.lag_phase) | copy-start | bytes 36868
  3.9 0.7 %copy-start.3 = (f32[2,2,512]{2,1,0:T(2,128)S(1)}, f32[2,2,512]{2,1,0:T(2,128)}, u32[]{:S(2)}) copy-start(f32[2,2,512]{2,1,0:T(2,128)} %constant.7.clone.share_phase) | copy-start | bytes 24580
  4.6 0.7 %copy-start.4 = (s32[4,4]{1,0:T(4,128)S(1)}, s32[4,4]{1,0:T(4,128)}, u32[]{:S(2)}) copy-start(s32[4,4]{1,0:T(4,128)} %pair.1) | copy-start | bytes 196
  5.3 0.7 %copy-start.5 = (s32[128]{0:T(128)S(1)}, s32[128]{0:T(128)}, u32[]{:S(2)}) copy-start(s32[128]{0:T(128)} %param.7) | copy-start | bytes 1540

commit v2 on v1

--- a/solution.py
+++ b/solution.py
@@ -93,20 +93,24 @@
     fetch.start()
 
     barrier = pltpu.get_barrier_semaphore()
-    peers = 0
-    for dc in range(C):
-        for dt in range(T):
-            for db in range(B):
-                same = dc == 0 and (dt or db)
-                line = dc != 0 and dt == 0 and db == 0
-                corner = dc in (1, C - 1) and dt in (1, T - 1) and db == 0
-                if not (same or line or (corner and dc != 0 and dt != 0)):
-                    continue
-                peers += 1
+    peers = T * B - 1
+    for other in range(1, T * B):
+        dt, db = divmod(other, B)
+        pl.semaphore_signal(
+            barrier, inc=1, device_id={"tm": lax.rem(t + dt, T), "band": lax.rem(b + db, B)},
+            device_id_type=pl.DeviceIdType.MESH,
+        )
+    for dc in [x for x in range(1 - C, C) if x]:
+        for dt in (-1, 0, 1) if abs(dc) == 1 else (0,):
+            there = (c + dc >= 0) & (c + dc < C) & (t + dt >= 0) & (t + dt < T)
+            peers = peers + there.astype(jnp.int32)
+
+            @pl.when(there)
+            def _():
                 pl.semaphore_signal(
                     barrier, inc=1,
                     device_id={
-                        "chan": lax.rem(c + dc, C), "tm": lax.rem(t + dt, T), "band": lax.rem(b + db, B)
+                        "chan": jnp.clip(c + dc, 0, C - 1), "tm": jnp.clip(t + dt, 0, T - 1)
                     },
                     device_id_type=pl.DeviceIdType.MESH,
                 )
@@ -256,10 +260,27 @@
     mine_white = (spectra * lax.rsqrt(power * (1.0 / kept) + 1e-06)).astype(BF)
     white[c, own] = mine_white
 
-    order = [d for pair_d in zip(range(1, C), range(C - 1, 0, -1)) for d in pair_d]
-    order = list(dict.fromkeys(order))
-    for dc in order:
-        start(white.at[c, own], white.at[c, own], z_sem.at[c], {"chan": lax.rem(c + dc, C)})
+    up, down = jnp.minimum(c + 1, C - 1), jnp.maximum(c - 1, 0)
+    for n in range(1, C):
+        for sign in (-1, 1):
+            to = c + sign * n
+            start(
+                white.at[c, own], white.at[c, own], z_sem.at[c],
+                {"chan": jnp.clip(to, 0, C - 1)}, (to >= 0) & (to < C),
+            )
+
+    def block_at(n, sign):
+        block = c + sign * n
+        return (block >= 0) & (block < C), jnp.clip(block, 0, C - 1)
+
+    def across(n, sign):
+        there, p = block_at(n, sign)
+        for dt in range(1, T):
+            tt = lax.rem(t + dt, T)
+            piece = white.at[p, tt * B + b]
+            arrived(piece, piece, x_sem.at[p, tt], there)
+            start(piece, piece, c_sem.at[p, tt], {"band": 1 - b}, there)
+
     w = mine_white.astype(F32)
     wr, wi = w[:, :kept], w[:, kept:]
     left = []
@@ -268,26 +289,28 @@
         sin_l = lag_phase[lag, 1:2, :]
         left.append(jnp.concatenate([wr * cos_l - wi * sin_l, wr * sin_l + wi * cos_l], axis=1))
     left = jnp.concatenate(left, axis=0).astype(BF)
-    for dc in order:
-        p = lax.rem(c + dc, C)
-        arrived(white.at[p, own], white.at[p, own], z_sem.at[p])
-        for dt in range(1, T):
-            start(
-                white.at[p, own], white.at[p, own], x_sem.at[p, t], {"tm": lax.rem(t + dt, T)}
-            )
-        start(white.at[p, own], white.at[p, own], c_sem.at[p, t], {"band": 1 - b})
-    for dc in order:
-        p = lax.rem(c + dc, C)
-        for dt in range(1, T):
-            tt = lax.rem(t + dt, T)
-            at = tt * B + b
-            arrived(white.at[p, at], white.at[p, at], x_sem.at[p, tt])
-            start(white.at[p, at], white.at[p, at], c_sem.at[p, tt], {"band": 1 - b})
-    for dc in order:
-        p = lax.rem(c + dc, C)
+    steps = [(n, sign) for n in range(1, C) for sign in (-1, 1)]
+    for n in range(1, C):
+        for sign in (-1, 1):
+            there, p = block_at(n, sign)
+            piece = white.at[p, own]
+            arrived(piece, piece, z_sem.at[p], there)
+            for dt in range(1, T):
+                start(piece, piece, x_sem.at[p, t], {"tm": lax.rem(t + dt, T)}, there)
+            start(piece, piece, c_sem.at[p, t], {"band": 1 - b}, there)
+        if n > 2:
+            for sign in (-1, 1):
+                across(n - 2, sign)
+    for sign in (-1, 1):
+        if C > 2:
+            across(C - 2, sign)
+    for sign in (-1, 1):
+        across(C - 1, sign)
+    for n, sign in steps:
+        there, p = block_at(n, sign)
         for tt in range(T):
-            at = tt * B + (1 - b)
-            arrived(white.at[p, at], white.at[p, at], c_sem.at[p, tt])
+            piece = white.at[p, tt * B + (1 - b)]
+            arrived(piece, piece, c_sem.at[p, tt], there)
 
     scale = 1.0 / math.sqrt(kept)
     for q in range(QMAX):
@@ -318,8 +341,7 @@
     rows = BLK // (T * B)
     table, share_phase, lag_phase = tables(samples, all_samples)
     vmem = pl.BlockSpec(memory_space=pltpu.VMEM)
-    n_send = 3 + 2 + T + (C - 1) * (1 + T + T) + 4
-    need = table.nbytes + C * BLK * 2 * kept * 2
+    n_send = 5 + T + 2 + 2 * (C - 1) * 2 * T
     return pl.pallas_call(
         functools.partial(kernel, C, T, B),
         out_shape=jax.ShapeDtypeStruct((1, QMAX, LAGS, rows, BLK), F32),
@@ -350,7 +372,7 @@
             pltpu.SemaphoreType.DMA((C, T)),
         ],
         compiler_params=pltpu.CompilerParams(
-            collective_id=0, has_side_effects=True, vmem_limit_bytes=need + (20 << 20)
+            collective_id=0, has_side_effects=True, vmem_limit_bytes=61 << 20
         ),
     )(
         recording, tau_index.reshape(1, channels), pair_offset,

time: 39.9 us -> 34.9 us (0.87)
  local copies, waits for them, and re-layouts: 6.65 us -> 1.62 us
    unnamed x13 -> x1, local copies, waits for them, and re-layouts: 6.65 us -> 1.62 us
where the time goes in v2:
time: 34.9 us; the launch traced here: 34.7 us
  Pallas kernels  33.1 us (95%)
  local copies, waits for them, and re-layouts  1.62 us (5%)
    pallas_call x1, Pallas kernels, shards(): pl.pallas_call(functools.partial(kernel, C, T, B), out_shape=jax.ShapeDty...  33.1 us
    unnamed x1, local copies, waits for them, and re-layouts  1.62 us

profile of v2, /device:TPU:3, one launch (start us, length us, event | category | flops | bytes accessed | tf_op | source)
XLA Modules:
  0.0 34.7 jit_solution(16322012478854676755)
XLA Ops:
  0.0 33.1 %shard_map.64 = f32[1,4,3,32,128]{4,3,2,1,0:T(8,128)} custom-call(f32[128,1024]{1,0:T(8,128)} %rec.1, s32[1,128]{1,0:T(1,128)} %bitcast.1, s32[4,4]{1,0:T(4,128)} %pair.1, bf16[2,1024,1024]{2,1,0:T(8,128)(2,1)} %constant.6.clone.table_hbm, f32[2,2,512]{2,1,0:T(2,128)} %constant.7.clone.share_phase, f32[3,2,512]{2,1,0:T(2,128)} %constant.8.clone.lag_phase), custom_call_target="tpu_custom_call" | custom-call | tf_op jit(solution)/shard_map/pallas_call | solution.py:345
  33.1 1.6 %copy.8 = f32[1,4,3,32,128]{4,3,2,1,0:T(8,128)} copy(f32[1,4,3,32,128]{4,3,2,1,0:T(8,128)} %shard_map.64) | data formatting | bytes 393216

commit v3 on v2

--- a/solution.py
+++ b/solution.py
@@ -100,7 +100,7 @@
             barrier, inc=1, device_id={"tm": lax.rem(t + dt, T), "band": lax.rem(b + db, B)},
             device_id_type=pl.DeviceIdType.MESH,
         )
-    for dc in [x for x in range(1 - C, C) if x]:
+    for dc in (-2, -1, 1, 2):
         for dt in (-1, 0, 1) if abs(dc) == 1 else (0,):
             there = (c + dc >= 0) & (c + dc < C) & (t + dt >= 0) & (t + dt < T)
             peers = peers + there.astype(jnp.int32)
@@ -208,13 +208,18 @@
         time_sem.at[1], {"tm": t_prev}, has_prev,
     )
 
-    def normed_block(n):
-        at = n * OUT_T
-        amp = dot(wide[:, at : at + OUT_T + 2 * HALO_T], window)
-        return filt[:, at : at + OUT_T] / (amp * (1.0 / WIN) + 1e-06)
+    def normed_blocks(which):
+        reach = OUT_T + 2 * HALO_T
+        stacked = jnp.concatenate([wide[:, n * OUT_T : n * OUT_T + reach] for n in which], axis=0)
+        amp = dot(stacked, window)
+        return [
+            filt[:, n * OUT_T : (n + 1) * OUT_T]
+            / (amp[at * half : (at + 1) * half] * (1.0 / WIN) + 1e-06)
+            for at, n in enumerate(which)
+        ]
 
     blocks = samples // OUT_T
-    inner = [normed_block(n) for n in range(1, blocks - 1)]
+    inner = normed_blocks(range(1, blocks - 1))
     fetch.wait()
     arrived(
         wide.at[:, pl.ds(samples, HALO_T)], wide.at[:, pl.ds(0, HALO_T)], time_sem.at[0], has_prev
@@ -223,7 +228,8 @@
         wide.at[:, pl.ds(HALO_T, HALO_T)], wide.at[:, pl.ds(HALO_T + samples, HALO_T)],
         time_sem.at[1], has_next,
     )
-    normed = jnp.concatenate([normed_block(0)] + inner + [normed_block(blocks - 1)], axis=1)
+    first_block, last_block = normed_blocks((0, blocks - 1))
+    normed = jnp.concatenate([first_block] + inner + [last_block], axis=1)
     n_high, n_low = split(normed)
     both = dot(jnp.concatenate([n_high, n_low], axis=0), table[0])
     spectrum = both[:half] + both[half:] + dot(n_high, table[1])
@@ -260,26 +266,33 @@
     mine_white = (spectra * lax.rsqrt(power * (1.0 / kept) + 1e-06)).astype(BF)
     white[c, own] = mine_white
 
-    up, down = jnp.minimum(c + 1, C - 1), jnp.maximum(c - 1, 0)
-    for n in range(1, C):
-        for sign in (-1, 1):
-            to = c + sign * n
-            start(
-                white.at[c, own], white.at[c, own], z_sem.at[c],
-                {"chan": jnp.clip(to, 0, C - 1)}, (to >= 0) & (to < C),
-            )
+    def half_of(p, at, h):
+        return white.at[p, at, :, pl.ds(h * kept, kept)]
 
     def block_at(n, sign):
         block = c + sign * n
         return (block >= 0) & (block < C), jnp.clip(block, 0, C - 1)
 
-    def across(n, sign):
+    for n in (2, 1):
+        for h in range(2):
+            for sign in (-1, 1):
+                there, to = block_at(n, sign)
+                piece = half_of(c, own, h)
+                start(piece, piece, z_sem.at[h, c], {"chan": to}, there)
+
+    def pass_on(p, sign, h, there):
+        piece = half_of(p, own, h)
+        goes = (c < C - 1) if sign < 0 else (c > 0)
+        to = jnp.clip(c - sign, 0, C - 1)
+        start(piece, piece, z_sem.at[h, p], {"chan": to}, there & goes)
+
+    def across(n, sign, h):
         there, p = block_at(n, sign)
         for dt in range(1, T):
             tt = lax.rem(t + dt, T)
-            piece = white.at[p, tt * B + b]
-            arrived(piece, piece, x_sem.at[p, tt], there)
-            start(piece, piece, c_sem.at[p, tt], {"band": 1 - b}, there)
+            piece = half_of(p, tt * B + b, h)
+            arrived(piece, piece, x_sem.at[h, p, tt], there)
+            start(piece, piece, c_sem.at[h, p, tt], {"band": 1 - b}, there)
 
     w = mine_white.astype(F32)
     wr, wi = w[:, :kept], w[:, kept:]
@@ -289,37 +302,35 @@
         sin_l = lag_phase[lag, 1:2, :]
         left.append(jnp.concatenate([wr * cos_l - wi * sin_l, wr * sin_l + wi * cos_l], axis=1))
     left = jnp.concatenate(left, axis=0).astype(BF)
-    steps = [(n, sign) for n in range(1, C) for sign in (-1, 1)]
-    for n in range(1, C):
-        for sign in (-1, 1):
-            there, p = block_at(n, sign)
-            piece = white.at[p, own]
-            arrived(piece, piece, z_sem.at[p], there)
-            for dt in range(1, T):
-                start(piece, piece, x_sem.at[p, t], {"tm": lax.rem(t + dt, T)}, there)
-            start(piece, piece, c_sem.at[p, t], {"band": 1 - b}, there)
-        if n > 2:
-            for sign in (-1, 1):
-                across(n - 2, sign)
-    for sign in (-1, 1):
-        if C > 2:
-            across(C - 2, sign)
-    for sign in (-1, 1):
-        across(C - 1, sign)
-    for n, sign in steps:
+    steps = [(n, h, sign) for n in [2, 1, *range(3, C)] for h in range(2) for sign in (-1, 1)]
+    late = 8
+    for at, (n, h, sign) in enumerate(steps):
+        there, p = block_at(n, sign)
+        piece = half_of(p, own, h)
+        arrived(piece, piece, z_sem.at[h, p], there)
+        if 2 <= n < C - 1:
+            pass_on(p, sign, h, there)
+        for dt in range(1, T):
+            start(piece, piece, x_sem.at[h, p, t], {"tm": lax.rem(t + dt, T)}, there)
+        start(piece, piece, c_sem.at[h, p, t], {"band": 1 - b}, there)
+        if at >= late:
+            n, h, sign = steps[at - late]
+            across(n, sign, h)
+    for n, h, sign in steps[max(len(steps) - late, 0):]:
+        across(n, sign, h)
+    for n, h, sign in steps:
         there, p = block_at(n, sign)
         for tt in range(T):
-            piece = white.at[p, tt * B + (1 - b)]
-            arrived(piece, piece, c_sem.at[p, tt], there)
-
-    scale = 1.0 / math.sqrt(kept)
+            piece = half_of(p, tt * B + (1 - b), h)
+            arrived(piece, piece, c_sem.at[h, p, tt], there)
+
     for q in range(QMAX):
         offset = pair[c, q]
         present = offset >= 0
         p = lax.rem(c + jnp.where(present, offset, 1), C)
         right = white[p].reshape(BLK, 2 * kept)
         product = lax.dot_general(left, right, NT, preferred_element_type=F32)
-        product = jnp.where(present, product * scale, 0.0)
+        product = jnp.where(present, product, 0.0)
         for lag in range(LAGS):
             out[0, q, lag] = product[lag * rows : (lag + 1) * rows]
 
@@ -341,8 +352,8 @@
     rows = BLK // (T * B)
     table, share_phase, lag_phase = tables(samples, all_samples)
     vmem = pl.BlockSpec(memory_space=pltpu.VMEM)
-    n_send = 5 + T + 2 + 2 * (C - 1) * 2 * T
-    return pl.pallas_call(
+    n_send = 5 + T + 4 * (C - 1) * (2 * T)
+    products = pl.pallas_call(
         functools.partial(kernel, C, T, B),
         out_shape=jax.ShapeDtypeStruct((1, QMAX, LAGS, rows, BLK), F32),
         in_specs=[
@@ -367,9 +378,9 @@
             pltpu.SemaphoreType.DMA((3,)),
             pltpu.SemaphoreType.DMA((2,)),
             pltpu.SemaphoreType.DMA((T,)),
-            pltpu.SemaphoreType.DMA((C,)),
-            pltpu.SemaphoreType.DMA((C, T)),
-            pltpu.SemaphoreType.DMA((C, T)),
+            pltpu.SemaphoreType.DMA((2, C)),
+            pltpu.SemaphoreType.DMA((2, C, T)),
+            pltpu.SemaphoreType.DMA((2, C, T)),
         ],
         compiler_params=pltpu.CompilerParams(
             collective_id=0, has_side_effects=True, vmem_limit_bytes=61 << 20
@@ -378,6 +389,7 @@
         recording, tau_index.reshape(1, channels), pair_offset,
         jnp.asarray(table), jnp.asarray(share_phase), jnp.asarray(lag_phase),
     )
+    return products * (1.0 / math.sqrt(kept))
 
 
 def solution(mesh):

time: 34.9 us -> 33.2 us (0.951)
  Pallas kernels: 33.1 us -> 31.1 us
  other arithmetic: 0 us -> 1.62 us
  local copies, waits for them, and re-layouts: 1.62 us -> 0 us
    pallas_call x1, Pallas kernels: 33.1 us -> 31.1 us  [shards(): pl.pallas_call(functools.partial(kernel, C, T, B), out_shape=jax.ShapeDty...]
    mul x0 -> x1, other arithmetic: none -> 1.62 us  [shards(): return products * (1.0 / math.sqrt(kept))]
    unnamed x1 -> x0, local copies, waits for them, and re-layouts: 1.62 us -> none
where the time goes in v3:
time: 33.2 us; the launch traced here: 32.8 us
  Pallas kernels  31.1 us (94%)
  other arithmetic  1.62 us (5%)
    pallas_call x1, Pallas kernels, shards(): pl.pallas_call(functools.partial(kernel, C, T, B), out_shape=jax.ShapeDty...  31.1 us
    mul x1, other arithmetic, shards(): return products * (1.0 / math.sqrt(kept))  1.62 us

profile of v3, /device:TPU:3, one launch (start us, length us, event | category | flops | bytes accessed | tf_op | source)
XLA Modules:
  0.0 32.8 jit_solution(4505400696339719244)
XLA Ops:
  0.0 31.1 %shard_map.64 = f32[1,4,3,32,128]{4,3,2,1,0:T(8,128)} custom-call(f32[128,1024]{1,0:T(8,128)} %rec.1, s32[1,128]{1,0:T(1,128)} %bitcast.1, s32[4,4]{1,0:T(4,128)} %pair.1, bf16[2,1024,1024]{2,1,0:T(8,128)(2,1)} %constant.8.clone.table_hbm, f32[2,2,512]{2,1,0:T(2,128)} %constant.9.clone.share_phase, f32[3,2,512]{2,1,0:T(2,128)} %constant.10.clone.lag_phase), custom_call_target="tpu_custom_call" | custom-call | tf_op jit(solution)/shard_map/pallas_call | solution.py:356
  31.2 1.6 %broadcast_multiply_fusion = f32[1,4,3,32,128]{4,3,2,1,0:T(8,128)} fusion(f32[1,4,3,32,128]{4,3,2,1,0:T(8,128)} %shard_map.64), kind=kLoop, calls=%fused_computation | loop fusion | flops 49152 | bytes 393216 | tf_op jit(solution)/shard_map/mul | solution.py:392

commit v4 on v3

--- a/solution.py
+++ b/solution.py
@@ -221,6 +221,14 @@
     blocks = samples // OUT_T
     inner = normed_blocks(range(1, blocks - 1))
     fetch.wait()
+
+    def transform(high, low, at):
+        size = high.shape[1]
+        both = dot(jnp.concatenate([high, low], axis=0), table[0, at : at + size])
+        return both[:half] + both[half:] + dot(high, table[1, at : at + size])
+
+    inner_high, inner_low = split(jnp.concatenate(inner, axis=1))
+    spectrum = transform(inner_high, inner_low, OUT_T)
     arrived(
         wide.at[:, pl.ds(samples, HALO_T)], wide.at[:, pl.ds(0, HALO_T)], time_sem.at[0], has_prev
     )
@@ -229,10 +237,8 @@
         time_sem.at[1], has_next,
     )
     first_block, last_block = normed_blocks((0, blocks - 1))
-    normed = jnp.concatenate([first_block] + inner + [last_block], axis=1)
-    n_high, n_low = split(normed)
-    both = dot(jnp.concatenate([n_high, n_low], axis=0), table[0])
-    spectrum = both[:half] + both[half:] + dot(n_high, table[1])
+    spectrum = spectrum + transform(*split(first_block), 0)
+    spectrum = spectrum + transform(*split(last_block), samples - OUT_T)
     cos_t = share_phase[t, 0:1, :]
     sin_t = share_phase[t, 1:2, :]
     re, im = spectrum[:, :kept], spectrum[:, kept:]

time: 33.2 us -> 32.8 us (0.988)
  no operation moved by 1% of the time
where the time goes in v4:
time: 32.8 us; the launch traced here: 32.7 us
  Pallas kernels  31 us (95%)
  other arithmetic  1.62 us (5%)
    pallas_call x1, Pallas kernels, shards(): pl.pallas_call(functools.partial(kernel, C, T, B), out_shape=jax.ShapeDty...  31 us
    mul x1, other arithmetic, shards(): return products * (1.0 / math.sqrt(kept))  1.62 us

profile of v4, /device:TPU:3, one launch (start us, length us, event | category | flops | bytes accessed | tf_op | source)
XLA Modules:
  0.0 32.7 jit_solution(8976445504031070573)
XLA Ops:
  0.0 31.0 %shard_map.64 = f32[1,4,3,32,128]{4,3,2,1,0:T(8,128)} custom-call(f32[128,1024]{1,0:T(8,128)} %rec.1, s32[1,128]{1,0:T(1,128)} %bitcast.1, s32[4,4]{1,0:T(4,128)} %pair.1, bf16[2,1024,1024]{2,1,0:T(8,128)(2,1)} %constant.8.clone.table_hbm, f32[2,2,512]{2,1,0:T(2,128)} %constant.9.clone.share_phase, f32[3,2,512]{2,1,0:T(2,128)} %constant.10.clone.lag_phase), custom_call_target="tpu_custom_call" | custom-call | tf_op jit(solution)/shard_map/pallas_call | solution.py:362
  31.0 1.6 %broadcast_multiply_fusion = f32[1,4,3,32,128]{4,3,2,1,0:T(8,128)} fusion(f32[1,4,3,32,128]{4,3,2,1,0:T(8,128)} %shard_map.64), kind=kLoop, calls=%fused_computation | loop fusion | flops 49152 | bytes 393216 | tf_op jit(solution)/shard_map/mul | solution.py:398
